TPU v7x, 512 devices: a whole 4x4x16 slice. The times are simulated.
512 devices in a mesh: row: 32 (over x, z_lo, core), col: 16 (over z_hi, y).
Axes of the slice: x: 4, y: 4, z: 16 (z_hi: 4, z_lo: 4; z = z_hi * 4 + z_lo), core: 2. Of those that a mesh axis runs over, the one named last changes fastest.
Arguments:
- initial_block: float32 [64, 32768], P(None, ('row', 'col')), may hold values from -6 to 6
- matrix_tiles: float32 [32, 16, 4, 128, 128], P('row', 'col'), may hold values from -0.0625 to 0.0625
- tile_rows: int32 [32, 16, 4], P('row', 'col'), may hold values from 0 to 7
- tile_columns: int32 [32, 16, 4], P('row', 'col'), may hold values from 0 to 15
Outputs:
- basis: float32 [64, 32768], P(None, ('row', 'col'))
- rayleigh: float32 [64, 64], replicated
- residual: float32 [64, 32768], P(None, ('row', 'col'))
All inputs are finite; a program needn't handle non-finite values.
Results may differ from a plain program's by a relative error of at most 0.00018.
Values sent between devices are 32-bit elements; how exact they have to be, the bound alone decides.
No kernel may reach another device: no remote copies, remote signals or barrier semaphores. Data moves between devices by JAX's collectives and lax.ppermute only.
A program may use at most 64 MiB of HBM per device.

v0:
```python
import jax
import jax.numpy as jnp
from jax import lax
from jax.sharding import PartitionSpec as P

TILE = 128
ITERS = 4


step_size = 0.5
momentum = 0.4


def tile_products(row_part, column_part, device_tiles, which_rows, which_columns):
    highest = lax.Precision.HIGHEST
    block_size = row_part.shape[0]
    row_tiles = row_part.reshape(block_size, -1, TILE)
    column_tiles = column_part.reshape(block_size, -1, TILE)
    row_pick = jnp.take(row_tiles, which_rows, axis=1)
    column_pick = jnp.take(column_tiles, which_columns, axis=1)
    direct = jnp.einsum("knj,nij->kni", column_pick, device_tiles, precision=highest)
    mirrored = jnp.einsum("kni,nij->knj", row_pick, device_tiles, precision=highest)
    row_onehot = (
        which_rows[:, None] == jnp.arange(row_tiles.shape[1], dtype=jnp.int32)[None, :]
    ).astype(device_tiles.dtype)
    column_onehot = (
        which_columns[:, None] == jnp.arange(column_tiles.shape[1], dtype=jnp.int32)[None, :]
    ).astype(device_tiles.dtype)
    direct_sum = jnp.einsum("kni,ns->ksi", direct, row_onehot, precision=highest).reshape(
        block_size, -1
    )
    mirrored_sum = jnp.einsum("knj,ns->ksj", mirrored, column_onehot, precision=highest).reshape(
        block_size, -1
    )
    return (direct_sum, mirrored_sum)


def inverse_factor(intersection):
    factor = jnp.linalg.cholesky(intersection)
    identity = jnp.eye(intersection.shape[0], dtype=intersection.dtype)
    return jax.scipy.linalg.solve_triangular(factor, identity, lower=True)


def inner(left, right):
    return jnp.dot(left, right.T, precision=lax.Precision.HIGHEST)


def per_device(initial_block, matrix_tiles, tile_rows, tile_columns):
    highest = lax.Precision.HIGHEST
    device_tiles = matrix_tiles[0, 0]
    which_rows = tile_rows[0, 0]
    which_columns = tile_columns[0, 0]

    def apply_operator(vectors):
        row_part = lax.all_gather(vectors, "col", axis=1, tiled=True)
        column_part = lax.all_gather(vectors, "row", axis=1, tiled=True)
        direct, mirrored = tile_products(
            row_part, column_part, device_tiles, which_rows, which_columns
        )
        return lax.psum_scatter(direct, "col", scatter_dimension=1, tiled=True) + lax.psum_scatter(
            mirrored, "row", scatter_dimension=1, tiled=True
        )

    def grand_sum(parts):
        return lax.psum(parts, ("row", "col"))

    inverse = inverse_factor(grand_sum(inner(initial_block, initial_block)))
    basis = jnp.dot(inverse, initial_block, precision=highest)
    image = apply_operator(basis)
    search = jnp.zeros_like(basis)
    search_image = jnp.zeros_like(basis)
    for iteration in range(ITERS):
        rayleigh = grand_sum(inner(basis, image))
        residual = image - jnp.dot(rayleigh, basis, precision=highest)
        residual_image = apply_operator(residual)
        search = -step_size * residual + momentum * search
        search_image = -step_size * residual_image + momentum * search_image
        trial = basis + search
        trial_image = image + search_image
        intersection = grand_sum(inner(trial, trial))
        inverse = inverse_factor(intersection)
        basis = jnp.dot(inverse, trial, precision=highest)
        image = jnp.dot(inverse, trial_image, precision=highest)
    rayleigh = grand_sum(inner(basis, image))
    residual = image - jnp.dot(rayleigh, basis, precision=highest)
    return (basis, rayleigh, residual)


def solution(mesh):
    in_specs = (
        P(None, ("row", "col")),
        P("row", "col", None, None, None),
        P("row", "col", None),
        P("row", "col", None),
    )
    out_specs = (P(None, ("row", "col")), P(), P(None, ("row", "col")))
    return jax.shard_map(
        per_device, mesh=mesh, in_specs=in_specs, out_specs=out_specs, check_vma=False
    )
```

profile of v0, /device:TPU:1, one launch (start us, length us, event | category | flops | bytes accessed | tf_op | source)
XLA Modules:
  0.0 2356.3 jit_solution(16314692396620609572)
XLA Ops:
  8.0 1.0 fusion.147
  9.0 111.2 %psum.70 = f32[64,64]{0,1:T(8,128)S(1)} all-reduce(f32[64,64]{0,1:T(8,128)S(1)} %fusion.147), channel_id=1, replica_groups=mesh['row'=32,'col'=16] {'row','col'}, use_global_device_ids=true, to_apply=%region_0.0 | all-reduce | flops 4096 | bytes 32768 | tf_op jit(solution)/shard_map/psum | solution.py:65
  120.2 5.8 cholesky.89
  127.4 4.9 custom-call.9
  133.3 44.0 %all_gather.30 = f32[64,2048]{0,1:T(8,128)S(1)} all-gather(f32[64,64]{0,1:T(8,128)S(1)} %copy.69), channel_id=1, replica_groups=mesh['row'=32,'col'=16] {'row'}, dimensions={1}, use_global_device_ids=true | all-gather | bytes 540672 | tf_op jit(solution)/shard_map/all_gather | solution.py:56
  180.0 1.0 copy.162
  181.1 48.5 %all_gather.31 = f32[64,1024]{0,1:T(8,128)S(1)} all-gather(f32[64,64]{0,1:T(8,128)S(1)} %copy.69), channel_id=1, replica_groups=mesh['row'=32,'col'=16] {'col'}, dimensions={1}, use_global_device_ids=true | all-gather | bytes 278528 | tf_op jit(solution)/shard_map/all_gather | solution.py:55
  231.3 1.4 copy.163
  232.7 53.6 %reduce-scatter.31.cloned.1.call-done = f32[64,64]{1,0:T(8,128)} async-done(((f32[1024,64]{1,0:T(8,128)}), f32[64,64]{1,0:T(8,128)}) %reduce-scatter.31.cloned.1.call-update) | async-done | bytes 16400
  287.1 144.4 %reduce-scatter.33.cloned.1.call-done = f32[64,64]{1,0:T(8,128)} async-done(((f32[2048,64]{1,0:T(8,128)}), f32[64,64]{1,0:T(8,128)}) %reduce-scatter.33.cloned.1.call-update) | async-done | bytes 16400
  432.6 107.8 %psum.71 = f32[64,64]{1,0:T(8,128)S(1)} all-reduce(f32[64,64]{1,0:T(8,128)S(1)} %fusion.149), channel_id=1, replica_groups=mesh['row'=32,'col'=16] {'row','col'}, use_global_device_ids=true, to_apply=%region_5.10 | all-reduce | flops 4096 | bytes 32768 | tf_op jit(solution)/shard_map/psum | solution.py:65
  540.9 44.3 %all_gather.32 = f32[64,2048]{0,1:T(8,128)S(1)} all-gather(f32[64,64]{0,1:T(8,128)S(1)} %copy.79), channel_id=1, replica_groups=mesh['row'=32,'col'=16] {'row'}, dimensions={1}, use_global_device_ids=true | all-gather | bytes 540672 | tf_op jit(solution)/shard_map/all_gather | solution.py:56
  587.1 1.0 copy.164
  588.2 46.1 %all_gather.33 = f32[64,1024]{0,1:T(8,128)S(1)} all-gather(f32[64,64]{0,1:T(8,128)S(1)} %copy.79), channel_id=1, replica_groups=mesh['row'=32,'col'=16] {'col'}, dimensions={1}, use_global_device_ids=true | all-gather | bytes 278528 | tf_op jit(solution)/shard_map/all_gather | solution.py:55
  634.3 106.3 %psum.72 = f32[64,64]{0,1:T(8,128)S(1)} all-reduce(f32[64,64]{0,1:T(8,128)S(1)} %fusion.111), channel_id=1, replica_groups=mesh['row'=32,'col'=16] {'row','col'}, use_global_device_ids=true, to_apply=%region_6.11 | all-reduce | flops 4096 | bytes 32768 | tf_op jit(solution)/shard_map/psum | solution.py:65
  742.4 1.4 copy.165
  744.0 5.8 cholesky.100
  751.2 4.9 custom-call.10
  756.6 0.8 copy.147
  757.4 125.5 %reduce-scatter.37.cloned.1.call-done = f32[64,64]{1,0:T(8,128)} async-done(((f32[2048,64]{1,0:T(8,128)}), f32[64,64]{1,0:T(8,128)}) %reduce-scatter.37.cloned.1.call-update) | async-done | bytes 16400
  884.1 107.9 %psum.73 = f32[64,64]{1,0:T(8,128)S(1)} all-reduce(f32[64,64]{1,0:T(8,128)S(1)} %fusion.150), channel_id=1, replica_groups=mesh['row'=32,'col'=16] {'row','col'}, use_global_device_ids=true, to_apply=%region_9.14 | all-reduce | flops 4096 | bytes 32768 | tf_op jit(solution)/shard_map/psum | solution.py:65
  992.4 44.1 %all_gather.34 = f32[64,2048]{0,1:T(8,128)S(1)} all-gather(f32[64,64]{0,1:T(8,128)S(1)} %copy.89), channel_id=1, replica_groups=mesh['row'=32,'col'=16] {'row'}, dimensions={1}, use_global_device_ids=true | all-gather | bytes 540672 | tf_op jit(solution)/shard_map/all_gather | solution.py:56
  1038.4 1.0 copy.166
  1039.6 47.7 %all_gather.35 = f32[64,1024]{0,1:T(8,128)S(1)} all-gather(f32[64,64]{0,1:T(8,128)S(1)} %copy.89), channel_id=1, replica_groups=mesh['row'=32,'col'=16] {'col'}, dimensions={1}, use_global_device_ids=true | all-gather | bytes 278528 | tf_op jit(solution)/shard_map/all_gather | solution.py:55
  1087.3 103.9 %psum.74 = f32[64,64]{0,1:T(8,128)S(1)} all-reduce(f32[64,64]{0,1:T(8,128)S(1)} %fusion.142), channel_id=1, replica_groups=mesh['row'=32,'col'=16] {'row','col'}, use_global_device_ids=true, to_apply=%region_10.15 | all-reduce | flops 4096 | bytes 32768 | tf_op jit(solution)/shard_map/psum | solution.py:65
  1193.0 1.4 copy.167
  1194.4 5.8 cholesky.111
  1201.6 4.9 custom-call.11
  1207.8 127.0 %reduce-scatter.41.cloned.1.call-done = f32[64,64]{1,0:T(8,128)} async-done(((f32[2048,64]{1,0:T(8,128)}), f32[64,64]{1,0:T(8,128)}) %reduce-scatter.41.cloned.1.call-update) | async-done | bytes 16400
  1336.0 108.4 %psum.75 = f32[64,64]{1,0:T(8,128)S(1)} all-reduce(f32[64,64]{1,0:T(8,128)S(1)} %fusion.151), channel_id=1, replica_groups=mesh['row'=32,'col'=16] {'row','col'}, use_global_device_ids=true, to_apply=%region_13.18 | all-reduce | flops 4096 | bytes 32768 | tf_op jit(solution)/shard_map/psum | solution.py:65
  1444.8 44.0 %all_gather.36 = f32[64,2048]{0,1:T(8,128)S(1)} all-gather(f32[64,64]{0,1:T(8,128)S(1)} %copy.99), channel_id=1, replica_groups=mesh['row'=32,'col'=16] {'row'}, dimensions={1}, use_global_device_ids=true | all-gather | bytes 540672 | tf_op jit(solution)/shard_map/all_gather | solution.py:56
  1490.8 1.0 copy.168
  1491.9 49.9 %all_gather.37 = f32[64,1024]{0,1:T(8,128)S(1)} all-gather(f32[64,64]{0,1:T(8,128)S(1)} %copy.99), channel_id=1, replica_groups=mesh['row'=32,'col'=16] {'col'}, dimensions={1}, use_global_device_ids=true | all-gather | bytes 278528 | tf_op jit(solution)/shard_map/all_gather | solution.py:55
  1541.8 102.8 %psum.76 = f32[64,64]{0,1:T(8,128)S(1)} all-reduce(f32[64,64]{0,1:T(8,128)S(1)} %fusion.152), channel_id=1, replica_groups=mesh['row'=32,'col'=16] {'row','col'}, use_global_device_ids=true, to_apply=%region_14.19 | all-reduce | flops 4096 | bytes 32768 | tf_op jit(solution)/shard_map/psum | solution.py:65
  1646.4 1.4 copy.169
  1647.9 5.8 cholesky.122
  1655.0 4.9 custom-call.12
  1661.2 126.0 %reduce-scatter.45.cloned.1.call-done = f32[64,64]{1,0:T(8,128)} async-done(((f32[2048,64]{1,0:T(8,128)}), f32[64,64]{1,0:T(8,128)}) %reduce-scatter.45.cloned.1.call-update) | async-done | bytes 16400
  1788.4 108.4 %psum.77 = f32[64,64]{1,0:T(8,128)S(1)} all-reduce(f32[64,64]{1,0:T(8,128)S(1)} %fusion.154), channel_id=1, replica_groups=mesh['row'=32,'col'=16] {'row','col'}, use_global_device_ids=true, to_apply=%region_17.22 | all-reduce | flops 4096 | bytes 32768 | tf_op jit(solution)/shard_map/psum | solution.py:65
  1897.2 43.8 %all_gather.38 = f32[64,2048]{0,1:T(8,128)S(1)} all-gather(f32[64,64]{0,1:T(8,128)S(1)} %copy.109), channel_id=1, replica_groups=mesh['row'=32,'col'=16] {'row'}, dimensions={1}, use_global_device_ids=true | all-gather | bytes 540672 | tf_op jit(solution)/shard_map/all_gather | solution.py:56
  1942.9 1.0 copy.170
  1944.1 47.8 %all_gather.39 = f32[64,1024]{0,1:T(8,128)S(1)} all-gather(f32[64,64]{0,1:T(8,128)S(1)} %copy.109), channel_id=1, replica_groups=mesh['row'=32,'col'=16] {'col'}, dimensions={1}, use_global_device_ids=true | all-gather | bytes 278528 | tf_op jit(solution)/shard_map/all_gather | solution.py:55
  1991.9 104.3 %psum.78 = f32[64,64]{0,1:T(8,128)S(1)} all-reduce(f32[64,64]{0,1:T(8,128)S(1)} %fusion.145), channel_id=1, replica_groups=mesh['row'=32,'col'=16] {'row','col'}, use_global_device_ids=true, to_apply=%region_18.23 | all-reduce | flops 4096 | bytes 32768 | tf_op jit(solution)/shard_map/psum | solution.py:65
  2098.0 1.4 copy.171
  2099.4 5.8 cholesky.133
  2106.6 4.9 custom-call.13
  2112.8 127.0 %reduce-scatter.49.cloned.1.call-done = f32[64,64]{1,0:T(8,128)} async-done(((f32[2048,64]{1,0:T(8,128)}), f32[64,64]{1,0:T(8,128)}) %reduce-scatter.49.cloned.1.call-update) | async-done | bytes 16400
  2241.0 107.7 %psum.79 = f32[64,64]{1,0:T(8,128)S(1)} all-reduce(f32[64,64]{1,0:T(8,128)S(1)} %fusion.155), channel_id=1, replica_groups=mesh['row'=32,'col'=16] {'row','col'}, use_global_device_ids=true, to_apply=%region_21.26 | all-reduce | flops 4096 | bytes 32768 | tf_op jit(solution)/shard_map/psum | solution.py:65
  (151 shorter events, 41.5 us)
Async XLA Ops:
  7.2 171.1 %copy-start = (f32[1,1,4,128,128]{4,3,2,1,0:T(8,128)S(1)}, f32[1,1,4,128,128]{4,3,2,1,0:T(8,128)}, u32[]{:S(2)}) copy-start(f32[1,1,4,128,128]{4,3,2,1,0:T(8,128)} %param.12) | copy-start | bytes 786436
  7.2 0.8 copy-start.5
  7.2 279.1 %reduce-scatter.31.cloned.1.call-start = ((), (), s32[]{:S(2)}) async-start(), calls=%async_computation.10 | async-start | bytes 557056
  132.3 0.8 copy-start.1
  178.9 0.7 copy-start.4
  181.1 250.5 %reduce-scatter.33.cloned.1.call-start = ((), (), s32[]{:S(2)}) async-start(), calls=%async_computation.11 | async-start | bytes 1081344
  232.7 523.9 %reduce-scatter.35.cloned.1.call-start = ((), (), s32[]{:S(2)}) async-start(), calls=%async_computation.12 | async-start | bytes 557056
  588.1 294.7 %reduce-scatter.37.cloned.1.call-start = ((), (), s32[]{:S(2)}) async-start(), calls=%async_computation.13 | async-start | bytes 1081344
  743.8 463.1 %reduce-scatter.39.cloned.1.call-start = ((), (), s32[]{:S(2)}) async-start(), calls=%async_computation.14 | async-start | bytes 557056
  1039.5 295.3 %reduce-scatter.41.cloned.1.call-start = ((), (), s32[]{:S(2)}) async-start(), calls=%async_computation.15 | async-start | bytes 1081344
  1194.3 466.1 %reduce-scatter.43.cloned.1.call-start = ((), (), s32[]{:S(2)}) async-start(), calls=%async_computation.16 | async-start | bytes 557056
  1491.8 295.3 %reduce-scatter.45.cloned.1.call-start = ((), (), s32[]{:S(2)}) async-start(), calls=%async_computation.17 | async-start | bytes 1081344
  1647.8 464.1 %reduce-scatter.47.cloned.1.call-start = ((), (), s32[]{:S(2)}) async-start(), calls=%async_computation.18 | async-start | bytes 557056
  1944.0 295.8 %reduce-scatter.49.cloned.1.call-start = ((), (), s32[]{:S(2)}) async-start(), calls=%async_computation.19 | async-start | bytes 1081344
  2111.9 236.8 %copy-start.2 = (f32[64,64]{1,0:T(8,128)}, f32[64,64]{1,0:T(8,128)S(1)}, u32[]{:S(2)}) copy-start(f32[64,64]{1,0:T(8,128)S(1)} %fusion.144) | copy-start | bytes 49156
  2348.7 0.8 copy-start.3
Sparse Core Ops, SparseCore 0:
  181.2 105.0 reduce-scatter.30
  289.3 142.1 reduce-scatter.32
  588.3 103.0 reduce-scatter.34
  743.9 138.9 reduce-scatter.36
  1039.6 104.0 reduce-scatter.38
  1194.4 140.2 reduce-scatter.40
  1492.0 104.4 reduce-scatter.42
  1647.9 139.2 reduce-scatter.44
  1944.1 104.6 reduce-scatter.46
  2099.5 140.2 reduce-scatter.48
where the time goes:
time: 2360 us
  blocking collectives  1530 us (65%)
  waiting for transfers between devices  704 us (30%)
  other arithmetic  61.1 us (3%)
  local copies, waits for them, and re-layouts  30.3 us (1%)
    psum x10, blocking collectives, grand_sum(): return lax.psum(parts, ('row', 'col'))  1070 us
    unnamed x20, waiting for transfers between devices  704 us
    all_gather x5, blocking collectives, apply_operator(): row_part = lax.all_gather(vectors, 'col', axis=1, tiled=True)  240 us
    all_gather x5, blocking collectives, apply_operator(): column_part = lax.all_gather(vectors, 'row', axis=1, tiled=True)  220 us
  transfers between devices with their start and end apart: 10, of which 6 were waited for; matrix products, arithmetic and copies ran while one was open for 3% of the time, Pallas kernels for 0%

commit v1 on v0

v1 whole, which is shorter than its diff:
```python
import functools

import jax
import jax.numpy as jnp
from jax import lax
from jax.experimental import pallas as pl
from jax.experimental.pallas import tpu as pltpu
from jax.sharding import Mesh
from jax.sharding import PartitionSpec as P

TILE = 128
HALF = 64
VEC = 64
ITERS = 4
STEP = 0.5
MOMENTUM = 0.4
AXES = ("x", "zl", "core", "zh", "y")
ROW = ("x", "zl", "core")
COL = ("zh", "y")
SPLIT = (4, 4, 2, 4, 4)


def dot(a, b, contract=((1,), (0,))):
    return lax.dot_general(
        a,
        b,
        (contract, ((), ())),
        precision=lax.Precision.HIGHEST,
        preferred_element_type=jnp.float32,
    )


NT = ((1,), (1,))


def lanes(rows):
    return lax.broadcasted_iota(jnp.int32, (rows, TILE), 1)


def swap_halves(v):
    return pltpu.roll(v, HALF, 1)


def pack_pair(tile):
    low = lanes(VEC // 2) < HALF
    top, bottom = tile[: VEC // 2], tile[VEC // 2 :]
    even = jnp.where(low, top, swap_halves(bottom))
    odd = jnp.where(low, swap_halves(top), bottom)
    return even, odd


def unpack_pair(even, odd):
    low = lanes(VEC // 2) < HALF
    top = jnp.where(low, even, swap_halves(odd))
    bottom = jnp.where(low, swap_halves(even), odd)
    return top, bottom


def inverse_cholesky(packed):
    low = lanes(VEC // 2) < HALF
    row_id = lax.broadcasted_iota(jnp.int32, (VEC // 2, TILE), 0)
    col_id = lanes(VEC // 2)
    eye_top = jnp.where(col_id - HALF == row_id, 1.0, 0.0)
    eye_bottom = jnp.where(col_id - HALF == row_id + VEC // 2, 1.0, 0.0)
    top = jnp.where(low, packed, eye_top)
    bottom = jnp.where(low, swap_halves(packed), eye_bottom)
    groups = [top[8 * g : 8 * g + 8] for g in range(4)] + [bottom[8 * g : 8 * g + 8] for g in range(4)]
    sub = lax.broadcasted_iota(jnp.int32, (8, TILE), 0)
    lane = lax.broadcasted_iota(jnp.int32, (8, TILE), 1)
    for j in range(VEC):
        own, at = divmod(j, 8)
        pivot_row = jnp.broadcast_to(groups[own][at : at + 1, :], (8, TILE))
        scale = 1.0 / jnp.broadcast_to(pivot_row[:, j : j + 1], (8, TILE))
        scaled = pivot_row * scale
        for g in range(own, 8):
            if g == own and at == 7:
                continue
            factor = jnp.broadcast_to(groups[g][:, j : j + 1], (8, TILE))
            update = groups[g] - factor * scaled
            groups[g] = jnp.where(sub > at, update, groups[g]) if g == own else update
    out = []
    for g in range(8):
        diagonal = jnp.sum(jnp.where(lane == sub + 8 * g, groups[g], 0.0), axis=1, keepdims=True)
        out.append(jnp.where(lane >= HALF, groups[g] / jnp.sqrt(diagonal), 0.0))
    return jnp.concatenate(out, axis=0)


def unpack_square(packed):
    return jnp.concatenate([packed, swap_halves(packed)], axis=0)[:, :HALF]


def small_algebra(gq_ref, size):
    gram = gq_ref[0]
    projected = unpack_square(gq_ref[1])
    right = inverse_cholesky(gram)
    left = swap_halves(right)
    inverse = left[:, :HALF]
    rayleigh = dot(dot(inverse, projected), inverse, NT)
    mixed = right - dot(rayleigh, left)
    return left, right, mixed, rayleigh


def gather_chunks(recv_row_ref, gq, count):
    each = VEC // 2 // count
    for r in range(count):
        for which in range(2):
            gq[which, r * each : (r + 1) * each, :] = recv_row_ref[
                r, VEC // 2 + which * each : VEC // 2 + (which + 1) * each, :
            ]


def emit_products(
    n_row, n_col, q, factor, own_gram, tiles_ref, rows_ref, cols_ref, send_row_ref, send_y_ref, direct, mirrored, own
):
    row_tiles, col_tiles = n_col // 2, n_row // 2
    direct[...] = jnp.zeros_like(direct)
    mirrored[...] = jnp.zeros_like(mirrored)
    cross = jnp.zeros((VEC, VEC), jnp.float32)
    for t in range(tiles_ref.shape[0]):
        i, j = rows_ref[t], cols_ref[t]
        tile = tiles_ref[t]
        row_pick = q[i]
        column_pick = q[row_tiles + j]
        product = dot(column_pick, tile, NT)
        direct[i] += product
        mirrored[j] += dot(row_pick, tile)
        cross = cross + dot(product, row_pick, NT)
    gram, projected = own_gram(own)
    projected = projected + factor * (cross + cross.T)
    low = lanes(VEC // 2) < HALF
    each = VEC // 2 // n_row

    def pack_square(m):
        wide = jnp.concatenate([m, m], axis=1)
        return jnp.where(low, wide[: VEC // 2], wide[VEC // 2 :])

    gram, projected = pack_square(gram), pack_square(projected)
    for b in range(col_tiles):
        even, odd = pack_pair(mirrored[b])
        send_row_ref[2 * b, : VEC // 2, :] = even
        send_row_ref[2 * b + 1, : VEC // 2, :] = odd
    rest = send_row_ref.shape[1] - VEC // 2 - 2 * each
    for r in range(n_row):
        pieces = [gram[r * each : (r + 1) * each], projected[r * each : (r + 1) * each]]
        if rest:
            pieces.append(jnp.zeros((rest, TILE), jnp.float32))
        send_row_ref[r, VEC // 2 :, :] = jnp.concatenate(pieces, axis=0)
    n_y = send_y_ref.shape[0]
    for s in range(row_tiles):
        for c, block in zip((2 * s, 2 * s + 1), pack_pair(direct[s])):
            zh, y = c // n_y, c % n_y
            send_y_ref[y, zh * (VEC // 2) : (zh + 1) * (VEC // 2), :] = block


def unpack_gathered(recv_row_ref, recv_col_ref, n_row, n_col, out):
    n_y = recv_col_ref.shape[0]
    half = VEC // 2

    def col_block(c):
        zh, y = c // n_y, c % n_y
        return recv_col_ref[y, zh * half : (zh + 1) * half, :]

    for s in range(n_col // 2):
        top, bottom = unpack_pair(col_block(2 * s), col_block(2 * s + 1))
        out[s, :half, :] = top
        out[s, half:, :] = bottom
    for b in range(n_row // 2):
        top, bottom = unpack_pair(recv_row_ref[2 * b, :half, :], recv_row_ref[2 * b + 1, :half, :])
        out[n_col // 2 + b, :half, :] = top
        out[n_col // 2 + b, half:, :] = bottom


def own_mask(where_ref):
    return (lanes(VEC) // HALF) == where_ref[1]


def first_kernel(
    n_row, n_col, where_ref, rows_ref, cols_ref, tiles_ref, recv_row_ref, recv_col_ref,
    trial_ref, send_row_ref, send_y_ref, direct, mirrored,
):
    unpack_gathered(recv_row_ref, recv_col_ref, n_row, n_col, trial_ref)

    def own_gram(own):
        mine = trial_ref[where_ref[0]]
        return dot(jnp.where(own_mask(where_ref), mine, 0.0), mine, NT), jnp.zeros((VEC, VEC), jnp.float32)

    emit_products(
        n_row, n_col, trial_ref, 1.0, own_gram, tiles_ref, rows_ref, cols_ref, send_row_ref, send_y_ref, direct, mirrored, None
    )


def middle_kernel(first, n_row, n_col, *refs):
    refs = list(refs)
    where_ref, rows_ref, cols_ref, tiles_ref, recv_row_ref, recv_col_ref, trial_ref = refs[:7]
    refs = refs[7:]
    if not first:
        known_ref, search_ref, search_image_ref = refs[:3]
        refs = refs[3:]
    (
        new_trial_ref, new_known_ref, new_search_ref, new_search_image_ref, send_row_ref, send_y_ref,
        direct, mirrored, fresh, gq,
    ) = refs
    n_tiles = n_col // 2 + n_row // 2
    gather_chunks(recv_row_ref, gq, n_row)
    unpack_gathered(recv_row_ref, recv_col_ref, n_row, n_col, fresh)
    left, right, mixed, _ = small_algebra(gq, n_row)
    for t in range(n_tiles):
        image = fresh[t]
        trial = trial_ref[t]
        if first:
            search = None
            trial_image = image
        else:
            search_image = -STEP * image + MOMENTUM * search_image_ref[t]
            new_search_image_ref[t] = search_image
            trial_image = known_ref[t] - STEP * image
        both = jnp.concatenate([trial, trial_image], axis=0)
        basis = dot(left, both)
        new_image = dot(right, both)
        residual = dot(mixed, both)
        fresh[t] = residual
        if first:
            new_search = -STEP * residual
            new_known_ref[t] = new_image
            new_search_image_ref[t] = jnp.zeros_like(image)
        else:
            new_search = -STEP * residual + MOMENTUM * search_ref[t]
            new_known_ref[t] = new_image + MOMENTUM * search_image
        new_search_ref[t] = new_search
        new_trial_ref[t] = basis + new_search

    def own_gram(own):
        at = where_ref[0]
        mask = own_mask(where_ref)
        trial = jnp.where(mask, new_trial_ref[at], 0.0)
        known = jnp.where(mask, new_known_ref[at], 0.0)
        gram = dot(trial, trial, NT)
        projected = dot(trial, known, NT) - STEP * dot(known, fresh[at], NT)
        return gram, projected

    emit_products(
        n_row, n_col, fresh, STEP * STEP, own_gram, tiles_ref, rows_ref, cols_ref, send_row_ref, send_y_ref,
        direct, mirrored, None,
    )


def last_kernel(n_row, where_ref, recv_ref, local_ref, trial_ref, known_ref, basis_ref, rayleigh_ref, residual_ref, gq):
    each = VEC // 2 // n_row
    for r in range(n_row):
        for which in range(2):
            gq[which, r * each : (r + 1) * each, :] = recv_ref[r, which * each : (which + 1) * each, :]
    left, right, mixed, rayleigh = small_algebra(gq, n_row)
    block = local_ref[: VEC // 2, :]
    image = jnp.concatenate(unpack_pair(block, block), axis=0)
    trial = trial_ref[where_ref[0]]
    trial_image = known_ref[where_ref[0]] - STEP * image
    both = jnp.concatenate([trial, trial_image], axis=0)
    odd = where_ref[1] == 1
    basis = dot(left, both)
    residual = dot(mixed, both)
    basis_ref[...] = jnp.where(odd, swap_halves(basis), basis)[:, :HALF]
    residual_ref[...] = jnp.where(odd, swap_halves(residual), residual)[:, :HALF]
    rayleigh_ref[...] = rayleigh


def per_device(split, initial_block, matrix_tiles, tile_rows, tile_columns):
    n_x, n_zl, n_core, n_zh, n_y = split
    n_row, n_col = n_x * n_zl * n_core, n_zh * n_y
    n_tiles = n_row // 2 + n_col // 2
    half = VEC // 2
    each = half // n_row
    extra = -(-2 * each // 8) * 8
    tiles = matrix_tiles[0, 0]
    rows, cols = tile_rows[0, 0], tile_columns[0, 0]
    my_col = lax.axis_index("zh") * n_y + lax.axis_index("y")
    where = jnp.stack([my_col // 2, my_col % 2]).astype(jnp.int32)

    smem = pl.BlockSpec(memory_space=pltpu.SMEM)
    vmem = pl.BlockSpec(memory_space=pltpu.VMEM)
    f32 = jnp.float32
    state = jax.ShapeDtypeStruct((n_tiles, VEC, TILE), f32)
    send_row = jax.ShapeDtypeStruct((n_row, half + extra, TILE), f32)
    send_y = jax.ShapeDtypeStruct((n_y, n_zh * half, TILE), f32)
    params = pltpu.CompilerParams(vmem_limit_bytes=24 * 1024 * 1024)
    partial_sums = [pltpu.VMEM((n_col // 2, VEC, TILE), f32), pltpu.VMEM((n_row // 2, VEC, TILE), f32)]

    def exchange(blocks, axes):
        return lax.all_to_all(blocks, axes, 0, 0, tiled=True)

    def spread(block, axes, count):
        return exchange(jnp.broadcast_to(block[None], (count,) + block.shape), axes)

    def scatter(row_blocks, y_blocks):
        mirrored = jnp.sum(exchange(row_blocks, ROW), axis=0)
        sums = jnp.broadcast_to(mirrored[None, half:], (n_y, extra, TILE))
        along_y = jnp.sum(exchange(jnp.concatenate([y_blocks, sums], axis=1), "y"), axis=0)
        sums = jnp.broadcast_to(along_y[None, n_zh * half :], (n_zh, extra, TILE))
        blocks = along_y[: n_zh * half].reshape(n_zh, half, TILE)
        along_z = jnp.sum(exchange(jnp.concatenate([blocks, sums], axis=1), "zh"), axis=0)
        return jnp.concatenate([along_z[:half] + mirrored[:half], along_z[half:]], axis=0)

    def gather(block):
        along_z = spread(block[:half], "zh", n_zh)
        along_y = spread(along_z.reshape(n_zh * half, TILE), "y", n_y)
        return spread(block, ROW, n_row), along_y

    start = jnp.concatenate([initial_block[:half], initial_block[half:]], axis=1)
    start = jnp.concatenate([start, jnp.zeros((extra, TILE), f32)], axis=0)
    from_row, from_col = gather(start)
    trial, row_blocks, y_blocks = pl.pallas_call(
        functools.partial(first_kernel, n_row, n_col),
        out_shape=(state, send_row, send_y),
        in_specs=[smem] * 3 + [vmem] * 3,
        out_specs=(vmem,) * 3,
        scratch_shapes=partial_sums,
        compiler_params=params,
    )(where, rows, cols, tiles, from_row, from_col)
    carried = (trial,)
    for iteration in range(ITERS):
        from_row, from_col = gather(scatter(row_blocks, y_blocks))
        *carried, row_blocks, y_blocks = pl.pallas_call(
            functools.partial(middle_kernel, iteration == 0, n_row, n_col),
            out_shape=(state,) * 4 + (send_row, send_y),
            in_specs=[smem] * 3 + [vmem] * (3 + len(carried)),
            out_specs=(vmem,) * 6,
            scratch_shapes=partial_sums
            + [pltpu.VMEM((n_tiles, VEC, TILE), f32), pltpu.VMEM((2, half, TILE), f32)],
            compiler_params=params,
        )(where, rows, cols, tiles, from_row, from_col, *carried)
    trial, known = carried[:2]
    local = scatter(row_blocks, y_blocks)
    sums = spread(local[half:], ROW, n_row)
    small = jax.ShapeDtypeStruct((VEC, VEC), f32)
    return pl.pallas_call(
        functools.partial(last_kernel, n_row),
        out_shape=(small,) * 3,
        in_specs=[smem] + [vmem] * 4,
        out_specs=(vmem,) * 3,
        scratch_shapes=[pltpu.VMEM((2, half, TILE), f32)],
        compiler_params=params,
    )(where, sums, local, trial, known)


def solution(mesh, split=SPLIT):
    fine = Mesh(mesh.devices.reshape(split), AXES)
    in_specs = (
        P(None, AXES),
        P(ROW, COL, None, None, None),
        P(ROW, COL, None),
        P(ROW, COL, None),
    )
    out_specs = (P(None, AXES), P(), P(None, AXES))
    return jax.shard_map(
        functools.partial(per_device, split),
        mesh=fine,
        in_specs=in_specs,
        out_specs=out_specs,
        check_vma=False,
    )
```

time: 2360 us -> 621 us (0.26)
  blocking collectives: 1530 us -> 429 us
  waiting for transfers between devices: 704 us -> 55.6 us
  Pallas kernels: 0 us -> 71.9 us
  other arithmetic: 61.1 us -> 1.83 us
  starting transfers between devices: 0.6 us -> 33.7 us
    psum x10 -> x0, blocking collectives: 1070 us -> none  [grand_sum(): return lax.psum(parts, ('row', 'col'))]
    unnamed x20 -> x0, waiting for transfers between devices: 704 us -> none
    all_gather x10 -> x0, blocking collectives: 460 us -> none  [the longest x5 240 us: apply_operator(): row_part = lax.all_gather(vectors, 'col', axis=1, tiled=True)]
    all_to_all x0 -> x24, blocking collectives: none -> 429 us  [exchange(): return lax.all_to_all(blocks, axes, 0, 0, tiled=True)]
    pallas_call x0 -> x6, Pallas kernels: none -> 71.9 us  [the longest x4 59.4 us: per_device(): pl.pallas_call(functools.partial(middle_kernel, iteration == 0, n_row, n_...]
    another operation x25 -> x1, other arithmetic: 60.3 us -> 0.08 us  [per_device(): where = jnp.stack([my_col // 2, my_col % 2]).astype(jnp.int32)]
    all_to_all x0 -> x7, waiting for transfers between devices: none -> 55.6 us  [exchange(): return lax.all_to_all(blocks, axes, 0, 0, tiled=True)]
    all_to_all x0 -> x7, starting transfers between devices: none -> 33.7 us  [exchange(): return lax.all_to_all(blocks, axes, 0, 0, tiled=True)]
  transfers between devices with their start and end apart: 10 -> 7, of which waited for: 6 -> 7; matrix products, arithmetic and copies ran while one was open for 3% -> 0% of each run, Pallas kernels for 0% -> 0%
where the time goes in v1:
time: 621 us; the launch traced here: 611 us
  blocking collectives  429 us (69%)
  Pallas kernels  71.9 us (12%)
  waiting for transfers between devices  55.6 us (9%)
  starting transfers between devices  33.7 us (5%)
  local copies, waits for them, and re-layouts  18.1 us (3%)
    all_to_all x24, blocking collectives, exchange(): return lax.all_to_all(blocks, axes, 0, 0, tiled=True)  429 us
    pallas_call x4, Pallas kernels, per_device(): pl.pallas_call(functools.partial(middle_kernel, iteration == 0, n_row, n_...  59.4 us
    all_to_all x7, waiting for transfers between devices, exchange(): return lax.all_to_all(blocks, axes, 0, 0, tiled=True)  55.6 us
    all_to_all x7, starting transfers between devices, exchange(): return lax.all_to_all(blocks, axes, 0, 0, tiled=True)  33.7 us
  transfers between devices with their start and end apart: 7, of which 7 were waited for; matrix products, arithmetic and copies ran while one was open for 0% of the time, Pallas kernels for 0%

profile of v1, /device:TPU:1, one launch (start us, length us, event | category | flops | bytes accessed | tf_op | source)
XLA Modules:
  0.0 611.3 jit_solution(3891596030111070572)
XLA Ops:
  1.5 27.9 %all_to_all.155 = f32[4,32,128]{2,1,0:T(8,128)S(1)} all-to-all(f32[4,32,128]{2,1,0:T(8,128)S(1)} %broadcast_in_dim.63), channel_id=1, replica_groups=mesh['x'=4,'zl'=4,'core'=2,'zh'=4,'y'=4] {'zh'}, dimensions={0} | all-to-all | bytes 131072 | tf_op jit(solution)/shard_map/all_to_all | solution.py:288
  30.1 4.2 all-to-all-start.2
  34.3 5.5 all-to-all-done.2.recv_col_ref
  40.7 9.4 %all-to-all-start = ((f32[32,40,128]{2,1,0:T(8,128)}), f32[32,40,128]{2,1,0:T(8,128)S(1)}, u32[]{:S(2)}, u32[]{:S(2)}) async-start(f32[32,40,128]{2,1,0:T(8,128)} %broadcast_in_dim.62), calls=%async_computation | async-start | bytes 1310720 | tf_op jit(solution)/shard_map/all_to_all | solution.py:288
  50.2 19.5 %all-to-all-done.recv_row_ref = f32[32,40,128]{2,1,0:T(8,128)S(1)} async-done(((f32[32,40,128]{2,1,0:T(8,128)}), f32[32,40,128]{2,1,0:T(8,128)S(1)}, u32[]{:S(2)}, u32[]{:S(2)}) %all-to-all-start) | async-done | bytes 655392 | tf_op jit(solution)/shard_map/all_to_all | solution.py:288
  70.4 2.2 shard_map.67
  72.6 23.1 %all_to_all.156 = f32[32,40,128]{2,1,0:T(8,128)S(1)} all-to-all(f32[32,40,128]{2,1,0:T(8,128)S(1)} %get-tuple-element.29), channel_id=1, replica_groups=mesh['x'=4,'zl'=4,'core'=2,'zh'=4,'y'=4] {'x','zl','core'}, dimensions={0} | all-to-all | bytes 1310720 | tf_op jit(solution)/shard_map/all_to_all | solution.py:288
  95.8 8.9 %all_to_all.157 = f32[4,136,128]{2,1,0:T(8,128)S(1)} all-to-all(f32[4,136,128]{2,1,0:T(8,128)S(1)} %pad_maximum_fusion), channel_id=1, replica_groups=mesh['x'=4,'zl'=4,'core'=2,'zh'=4,'y'=4] {'y'}, dimensions={0} | all-to-all | bytes 557056 | tf_op jit(solution)/shard_map/all_to_all | solution.py:288
  104.7 14.2 %all_to_all.158 = f32[4,40,128]{2,1,0:T(8,128)S(1)} all-to-all(f32[4,40,128]{2,1,0:T(8,128)S(1)} %pad_maximum_fusion.5), channel_id=1, replica_groups=mesh['x'=4,'zl'=4,'core'=2,'zh'=4,'y'=4] {'zh'}, dimensions={0} | all-to-all | bytes 163840 | tf_op jit(solution)/shard_map/all_to_all | solution.py:288
  118.9 14.7 %all_to_all.159 = f32[4,32,128]{2,1,0:T(8,128)S(1)} all-to-all(f32[4,32,128]{2,1,0:T(8,128)S(1)} %broadcast_in_dim.69), channel_id=1, replica_groups=mesh['x'=4,'zl'=4,'core'=2,'zh'=4,'y'=4] {'zh'}, dimensions={0} | all-to-all | bytes 131072 | tf_op jit(solution)/shard_map/all_to_all | solution.py:288
  134.3 3.4 all-to-all-start.8
  137.7 5.5 all-to-all-done.8.refs_5_
  143.2 27.6 %all_to_all.160.refs_4_ = f32[32,40,128]{2,1,0:T(8,128)S(1)} all-to-all(f32[32,40,128]{2,1,0:T(8,128)S(1)} %broadcast_in_dim.68), channel_id=1, replica_groups=mesh['x'=4,'zl'=4,'core'=2,'zh'=4,'y'=4] {'x','zl','core'}, dimensions={0} | all-to-all | bytes 1310720 | tf_op jit(solution)/shard_map/all_to_all | solution.py:288
  170.9 14.6 %shard_map.68 = (f32[24,64,128]{2,1,0:T(8,128)S(1)}, f32[24,64,128]{2,1,0:T(8,128)S(1)}, f32[24,64,128]{2,1,0:T(8,128)S(1)}, f32[24,64,128]{2,1,0:T(8,128)S(1)},...) custom-call(s32[2]{0:T(128)S(1)} %pad_add_fusion.where_ref.refs_0_, s32[4]{0:T(128)S(1)} %bitcast.21, ...), custom_call_target="tpu_custom_call" | custom-call | tf_op jit(solution)/shard_map/pallas_call | solution.py:321
  187.3 0.9 copy-done.15
  189.1 23.1 %all_to_all.161 = f32[32,40,128]{2,1,0:T(8,128)S(1)} all-to-all(f32[32,40,128]{2,1,0:T(8,128)S(1)} %get-tuple-element.32), channel_id=1, replica_groups=mesh['x'=4,'zl'=4,'core'=2,'zh'=4,'y'=4] {'x','zl','core'}, dimensions={0} | all-to-all | bytes 1310720 | tf_op jit(solution)/shard_map/all_to_all | solution.py:288
  212.3 8.9 %all_to_all.162 = f32[4,136,128]{2,1,0:T(8,128)S(1)} all-to-all(f32[4,136,128]{2,1,0:T(8,128)S(1)} %pad_maximum_fusion.1), channel_id=1, replica_groups=mesh['x'=4,'zl'=4,'core'=2,'zh'=4,'y'=4] {'y'}, dimensions={0} | all-to-all | bytes 557056 | tf_op jit(solution)/shard_map/all_to_all | solution.py:288
  221.2 14.2 %all_to_all.163 = f32[4,40,128]{2,1,0:T(8,128)S(1)} all-to-all(f32[4,40,128]{2,1,0:T(8,128)S(1)} %pad_maximum_fusion.6), channel_id=1, replica_groups=mesh['x'=4,'zl'=4,'core'=2,'zh'=4,'y'=4] {'zh'}, dimensions={0} | all-to-all | bytes 163840 | tf_op jit(solution)/shard_map/all_to_all | solution.py:288
  235.4 14.7 %all_to_all.164 = f32[4,32,128]{2,1,0:T(8,128)S(1)} all-to-all(f32[4,32,128]{2,1,0:T(8,128)S(1)} %broadcast_in_dim.75), channel_id=1, replica_groups=mesh['x'=4,'zl'=4,'core'=2,'zh'=4,'y'=4] {'zh'}, dimensions={0} | all-to-all | bytes 131072 | tf_op jit(solution)/shard_map/all_to_all | solution.py:288
  250.8 3.4 all-to-all-start.14
  254.2 5.5 all-to-all-done.14.refs_5_
  259.8 27.8 %all_to_all.165.refs_4_ = f32[32,40,128]{2,1,0:T(8,128)S(1)} all-to-all(f32[32,40,128]{2,1,0:T(8,128)S(1)} %broadcast_in_dim.74), channel_id=1, replica_groups=mesh['x'=4,'zl'=4,'core'=2,'zh'=4,'y'=4] {'x','zl','core'}, dimensions={0} | all-to-all | bytes 1310720 | tf_op jit(solution)/shard_map/all_to_all | solution.py:288
  287.5 1.1 copy-done.16
  288.7 1.1 copy-done.18
  289.8 14.7 %shard_map.69 = (f32[24,64,128]{2,1,0:T(8,128)S(1)}, f32[24,64,128]{2,1,0:T(8,128)S(1)}, f32[24,64,128]{2,1,0:T(8,128)S(1)}, f32[24,64,128]{2,1,0:T(8,128)S(1)},...) custom-call(s32[2]{0:T(128)S(1)} %pad_add_fusion.where_ref.refs_0_, s32[4]{0:T(128)S(1)} %bitcast.22, ...), custom_call_target="tpu_custom_call" | custom-call | tf_op jit(solution)/shard_map/pallas_call | solution.py:321
  305.4 23.2 %all_to_all.166 = f32[32,40,128]{2,1,0:T(8,128)} all-to-all(f32[32,40,128]{2,1,0:T(8,128)S(1)} %get-tuple-element.38), channel_id=1, replica_groups=mesh['x'=4,'zl'=4,'core'=2,'zh'=4,'y'=4] {'x','zl','core'}, dimensions={0} | all-to-all | bytes 1310720 | tf_op jit(solution)/shard_map/all_to_all | solution.py:288
  328.6 1.1 reduce_sum.141
  329.8 8.9 %all_to_all.167 = f32[4,136,128]{2,1,0:T(8,128)S(1)} all-to-all(f32[4,136,128]{2,1,0:T(8,128)S(1)} %pad_maximum_fusion.2), channel_id=1, replica_groups=mesh['x'=4,'zl'=4,'core'=2,'zh'=4,'y'=4] {'y'}, dimensions={0} | all-to-all | bytes 557056 | tf_op jit(solution)/shard_map/all_to_all | solution.py:288
  338.7 14.2 %all_to_all.168 = f32[4,40,128]{2,1,0:T(8,128)S(1)} all-to-all(f32[4,40,128]{2,1,0:T(8,128)S(1)} %pad_maximum_fusion.7), channel_id=1, replica_groups=mesh['x'=4,'zl'=4,'core'=2,'zh'=4,'y'=4] {'zh'}, dimensions={0} | all-to-all | bytes 163840 | tf_op jit(solution)/shard_map/all_to_all | solution.py:288
  352.9 14.7 %all_to_all.169 = f32[4,32,128]{2,1,0:T(8,128)S(1)} all-to-all(f32[4,32,128]{2,1,0:T(8,128)S(1)} %broadcast_in_dim.81), channel_id=1, replica_groups=mesh['x'=4,'zl'=4,'core'=2,'zh'=4,'y'=4] {'zh'}, dimensions={0} | all-to-all | bytes 131072 | tf_op jit(solution)/shard_map/all_to_all | solution.py:288
  368.3 3.4 all-to-all-start.20
  371.8 5.5 all-to-all-done.20.refs_5_
  377.3 27.9 %all_to_all.170.refs_4_ = f32[32,40,128]{2,1,0:T(8,128)S(1)} all-to-all(f32[32,40,128]{2,1,0:T(8,128)S(1)} %broadcast_in_dim.80), channel_id=1, replica_groups=mesh['x'=4,'zl'=4,'core'=2,'zh'=4,'y'=4] {'x','zl','core'}, dimensions={0} | all-to-all | bytes 1310720 | tf_op jit(solution)/shard_map/all_to_all | solution.py:288
  405.2 14.7 %shard_map.70 = (f32[24,64,128]{2,1,0:T(8,128)S(1)}, f32[24,64,128]{2,1,0:T(8,128)S(1)}, f32[24,64,128]{2,1,0:T(8,128)S(1)}, f32[24,64,128]{2,1,0:T(8,128)S(1)},...) custom-call(s32[2]{0:T(128)S(1)} %pad_add_fusion.where_ref.refs_0_, s32[4]{0:T(128)S(1)} %bitcast.23, ...), custom_call_target="tpu_custom_call" | custom-call | tf_op jit(solution)/shard_map/pallas_call | solution.py:321
  423.5 23.1 %all_to_all.171 = f32[32,40,128]{2,1,0:T(8,128)S(1)} all-to-all(f32[32,40,128]{2,1,0:T(8,128)S(1)} %get-tuple-element.44), channel_id=1, replica_groups=mesh['x'=4,'zl'=4,'core'=2,'zh'=4,'y'=4] {'x','zl','core'}, dimensions={0} | all-to-all | bytes 1310720 | tf_op jit(solution)/shard_map/all_to_all | solution.py:288
  446.7 8.9 %all_to_all.172 = f32[4,136,128]{2,1,0:T(8,128)S(1)} all-to-all(f32[4,136,128]{2,1,0:T(8,128)S(1)} %pad_maximum_fusion.3), channel_id=1, replica_groups=mesh['x'=4,'zl'=4,'core'=2,'zh'=4,'y'=4] {'y'}, dimensions={0} | all-to-all | bytes 557056 | tf_op jit(solution)/shard_map/all_to_all | solution.py:288
  455.7 14.2 %all_to_all.173 = f32[4,40,128]{2,1,0:T(8,128)S(1)} all-to-all(f32[4,40,128]{2,1,0:T(8,128)S(1)} %pad_maximum_fusion.8), channel_id=1, replica_groups=mesh['x'=4,'zl'=4,'core'=2,'zh'=4,'y'=4] {'zh'}, dimensions={0} | all-to-all | bytes 163840 | tf_op jit(solution)/shard_map/all_to_all | solution.py:288
  469.9 14.8 %all_to_all.174 = f32[4,32,128]{2,1,0:T(8,128)S(1)} all-to-all(f32[4,32,128]{2,1,0:T(8,128)S(1)} %broadcast_in_dim.87), channel_id=1, replica_groups=mesh['x'=4,'zl'=4,'core'=2,'zh'=4,'y'=4] {'zh'}, dimensions={0} | all-to-all | bytes 131072 | tf_op jit(solution)/shard_map/all_to_all | solution.py:288
  485.4 3.5 all-to-all-start.26
  489.0 5.5 all-to-all-done.26.refs_5_
  494.5 27.9 %all_to_all.175.refs_4_ = f32[32,40,128]{2,1,0:T(8,128)S(1)} all-to-all(f32[32,40,128]{2,1,0:T(8,128)S(1)} %broadcast_in_dim.86), channel_id=1, replica_groups=mesh['x'=4,'zl'=4,'core'=2,'zh'=4,'y'=4] {'x','zl','core'}, dimensions={0} | all-to-all | bytes 1310720 | tf_op jit(solution)/shard_map/all_to_all | solution.py:288
  522.5 15.2 %shard_map.71 = (f32[24,64,128]{2,1,0:T(8,128)S(1)}, f32[24,64,128]{2,1,0:T(8,128)S(1)}, f32[24,64,128]{2,1,0:T(8,128)}, f32[24,64,128]{2,1,0:T(8,128)}, f32[32,...) custom-call(s32[2]{0:T(128)S(1)} %pad_add_fusion.where_ref.refs_0_, s32[4]{0:T(128)S(1)} %bitcast.24, s32[4]{0:T(128)S(1)} %bitcast.29, ...), custom_call_target="tpu_custom_call" | custom-call | tf_op jit(solution)/shard_map/pallas_call | solution.py:321
  538.6 23.1 %all_to_all.176 = f32[32,40,128]{2,1,0:T(8,128)S(1)} all-to-all(f32[32,40,128]{2,1,0:T(8,128)S(1)} %get-tuple-element.50), channel_id=1, replica_groups=mesh['x'=4,'zl'=4,'core'=2,'zh'=4,'y'=4] {'x','zl','core'}, dimensions={0} | all-to-all | bytes 1310720 | tf_op jit(solution)/shard_map/all_to_all | solution.py:288
  561.8 8.9 %all_to_all.177 = f32[4,136,128]{2,1,0:T(8,128)S(1)} all-to-all(f32[4,136,128]{2,1,0:T(8,128)S(1)} %pad_maximum_fusion.4), channel_id=1, replica_groups=mesh['x'=4,'zl'=4,'core'=2,'zh'=4,'y'=4] {'y'}, dimensions={0} | all-to-all | bytes 557056 | tf_op jit(solution)/shard_map/all_to_all | solution.py:288
  570.7 14.3 %all_to_all.178 = f32[4,40,128]{2,1,0:T(8,128)S(1)} all-to-all(f32[4,40,128]{2,1,0:T(8,128)S(1)} %pad_maximum_fusion.9), channel_id=1, replica_groups=mesh['x'=4,'zl'=4,'core'=2,'zh'=4,'y'=4] {'zh'}, dimensions={0} | all-to-all | bytes 163840 | tf_op jit(solution)/shard_map/all_to_all | solution.py:288
  585.7 6.3 %all-to-all-start.30 = ((f32[32,8,128]{2,1,0:T(8,128)}), f32[32,8,128]{2,1,0:T(8,128)S(1)}, u32[]{:S(2)}, u32[]{:S(2)}) async-start(f32[32,8,128]{2,1,0:T(8,128)} %broadcast_in_dim.92), calls=%async_computation.30 | async-start | bytes 262144 | tf_op jit(solution)/shard_map/all_to_all | solution.py:288
  592.0 8.7 %all-to-all-done.30.recv_ref = f32[32,8,128]{2,1,0:T(8,128)S(1)} async-done(((f32[32,8,128]{2,1,0:T(8,128)}), f32[32,8,128]{2,1,0:T(8,128)S(1)}, u32[]{:S(2)}, u32[]{:S(2)}) %all-to-all-start.30) | async-done | bytes 131104 | tf_op jit(solution)/shard_map/all_to_all | solution.py:288
  600.7 10.3 %shard_map.72 = (f32[64,64]{1,0:T(8,128)}, f32[64,64]{1,0:T(8,128)}, f32[64,64]{1,0:T(8,128)}) custom-call(s32[2]{0:T(128)S(1)} %pad_add_fusion.where_ref.refs_0_, f32[32,8,128]{2,1,0:T(8,128)S(1)} %all-to-all-done.30.recv_ref, f32[40,128]{1,0:T(8,128)S(1)} %pad_maximum_fusion.14.local_ref, f32[24,64,128]{2,1,0:T(8,128)S(1)} %get-tuple-element.51.trial_ref, ...), custom_call_target="tpu_custom_call" | custom-call | tf_op jit(solution)/shard_map/pallas_call | solution.py:334
  (127 shorter events, 15.6 us)
Async XLA Ops:
  30.1 9.7 %all-to-all-start.2 = ((f32[4,128,128]{2,1,0:T(8,128)}), f32[4,128,128]{2,1,0:T(8,128)S(1)}, u32[]{:S(2)}, u32[]{:S(2)}) async-start(f32[4,128,128]{2,1,0:T(8,128)} %broadcast_in_dim.65), calls=%async_computation.2 | async-start | bytes 524288 | tf_op jit(solution)/shard_map/all_to_all | solution.py:288
  40.7 29.0 %copy-start = (f32[1,1,4,128,128]{4,3,2,1,0:T(8,128)S(1)}, f32[1,1,4,128,128]{4,3,2,1,0:T(8,128)}, u32[]{:S(2)}) copy-start(f32[1,1,4,128,128]{4,3,2,1,0:T(8,128)} %param.5) | copy-start | bytes 786436
  40.7 29.0 %all-to-all-start = ((f32[32,40,128]{2,1,0:T(8,128)}), f32[32,40,128]{2,1,0:T(8,128)S(1)}, u32[]{:S(2)}, u32[]{:S(2)}) async-start(f32[32,40,128]{2,1,0:T(8,128)} %broadcast_in_dim.62), calls=%async_computation | async-start | bytes 1310720 | tf_op jit(solution)/shard_map/all_to_all | solution.py:288
  69.7 0.7 copy-start.21
  69.7 0.7 copy-start.22
  134.3 8.9 %all-to-all-start.8 = ((f32[4,128,128]{2,1,0:T(8,128)}), f32[4,128,128]{2,1,0:T(8,128)S(1)}, u32[]{:S(2)}, u32[]{:S(2)}) async-start(f32[4,128,128]{2,1,0:T(8,128)} %broadcast_in_dim.71), calls=%async_computation.8 | async-start | bytes 524288 | tf_op jit(solution)/shard_map/all_to_all | solution.py:288
  185.5 0.9 copy-start.11
  186.4 0.9 copy-start.13
  187.3 0.9 copy-start.15
  188.2 0.9 copy-start.17
  250.8 8.9 %all-to-all-start.14 = ((f32[4,128,128]{2,1,0:T(8,128)}), f32[4,128,128]{2,1,0:T(8,128)S(1)}, u32[]{:S(2)}, u32[]{:S(2)}) async-start(f32[4,128,128]{2,1,0:T(8,128)} %broadcast_in_dim.77), calls=%async_computation.14 | async-start | bytes 524288 | tf_op jit(solution)/shard_map/all_to_all | solution.py:288
  259.7 27.8 %copy-start.14 = (f32[24,64,128]{2,1,0:T(8,128)S(1)}, f32[24,64,128]{2,1,0:T(8,128)}, u32[]{:S(2)}) copy-start(f32[24,64,128]{2,1,0:T(8,128)} %copy-done.13) | copy-start | bytes 2359300
  259.8 27.8 %copy-start.12 = (f32[24,64,128]{2,1,0:T(8,128)S(1)}, f32[24,64,128]{2,1,0:T(8,128)}, u32[]{:S(2)}) copy-start(f32[24,64,128]{2,1,0:T(8,128)} %copy-done.11) | copy-start | bytes 2359300
  287.5 1.1 copy-start.16
  288.7 1.1 copy-start.18
  304.5 0.9 copy-start.1
  368.3 8.9 %all-to-all-start.20 = ((f32[4,128,128]{2,1,0:T(8,128)}), f32[4,128,128]{2,1,0:T(8,128)S(1)}, u32[]{:S(2)}, u32[]{:S(2)}) async-start(f32[4,128,128]{2,1,0:T(8,128)} %broadcast_in_dim.83), calls=%async_computation.20 | async-start | bytes 524288 | tf_op jit(solution)/shard_map/all_to_all | solution.py:288
  377.3 27.9 %copy-start.2 = (f32[24,64,128]{2,1,0:T(8,128)S(1)}, f32[24,64,128]{2,1,0:T(8,128)}, u32[]{:S(2)}) copy-start(f32[24,64,128]{2,1,0:T(8,128)} %copy-done.1) | copy-start | bytes 2359300
  420.0 0.9 copy-start.3
  420.8 0.9 copy-start.5
  421.7 0.9 copy-start.7
  422.6 0.9 copy-start.9
  469.8 52.6 %copy-start.10 = (f32[24,64,128]{2,1,0:T(8,128)S(1)}, f32[24,64,128]{2,1,0:T(8,128)}, u32[]{:S(2)}) copy-start(f32[24,64,128]{2,1,0:T(8,128)} %copy-done.9) | copy-start | bytes 2359300
  485.4 37.1 %copy-start.8 = (f32[24,64,128]{2,1,0:T(8,128)S(1)}, f32[24,64,128]{2,1,0:T(8,128)}, u32[]{:S(2)}) copy-start(f32[24,64,128]{2,1,0:T(8,128)} %copy-done.7) | copy-start | bytes 2359300
  485.4 9.0 %all-to-all-start.26 = ((f32[4,128,128]{2,1,0:T(8,128)}), f32[4,128,128]{2,1,0:T(8,128)S(1)}, u32[]{:S(2)}, u32[]{:S(2)}) async-start(f32[4,128,128]{2,1,0:T(8,128)} %broadcast_in_dim.89), calls=%async_computation.26 | async-start | bytes 524288 | tf_op jit(solution)/shard_map/all_to_all | solution.py:288
  494.4 28.0 %copy-start.6 = (f32[24,64,128]{2,1,0:T(8,128)S(1)}, f32[24,64,128]{2,1,0:T(8,128)}, u32[]{:S(2)}) copy-start(f32[24,64,128]{2,1,0:T(8,128)} %copy-done.5) | copy-start | bytes 2359300
  494.5 28.0 %copy-start.4 = (f32[24,64,128]{2,1,0:T(8,128)S(1)}, f32[24,64,128]{2,1,0:T(8,128)}, u32[]{:S(2)}) copy-start(f32[24,64,128]{2,1,0:T(8,128)} %copy-done.3) | copy-start | bytes 2359300
  537.7 0.9 copy-start.19
  570.7 30.1 %copy-start.20 = (f32[24,64,128]{2,1,0:T(8,128)S(1)}, f32[24,64,128]{2,1,0:T(8,128)}, u32[]{:S(2)}) copy-start(f32[24,64,128]{2,1,0:T(8,128)} %copy-done.19) | copy-start | bytes 2359300
  585.7 15.0 %all-to-all-start.30 = ((f32[32,8,128]{2,1,0:T(8,128)}), f32[32,8,128]{2,1,0:T(8,128)S(1)}, u32[]{:S(2)}, u32[]{:S(2)}) async-start(f32[32,8,128]{2,1,0:T(8,128)} %broadcast_in_dim.92), calls=%async_computation.30 | async-start | bytes 262144 | tf_op jit(solution)/shard_map/all_to_all | solution.py:288
